TPU v7x, 32 devices: a whole 2x2x4 slice. The times are simulated.
32 devices in a mesh: batch: 16 (over z, y, core), heads: 2 (over x).
Axes of the slice: x: 2, y: 2, z: 4, core: 2. Of those that a mesh axis runs over, the one named last changes fastest.
Arguments:
- token_ids: int32 [128, 2, 5], P('batch'), may hold values from 0 to 65535
- accepted: int32 [128], P('batch'), may hold values from 0 to 4
- lengths: int32 [128], P('batch'), may hold values from 128 to 512
- queries: bfloat16 [128, 2, 5, 4096], P('batch', None, None, 'heads'), may hold values from -8 to 8
- new_kv: bfloat16 [128, 2, 2, 5, 1024], P('batch', None, None, None, 'heads'), may hold values from -4 to 4
- cache_kv: bfloat16 [128, 2, 512, 1024], P('batch', None, None, 'heads'), may hold values from -8 to 8
- table: bfloat16 [65536, 8192], P('heads', 'batch'), may hold values from -6 to 6
- w_out: bfloat16 [4096, 8192], P('heads', 'batch'), may hold values from -0.1875 to 0.1875
- gain: float32 [8192], P('batch'), may hold values from 0.25 to 1.75
- w_feat: bfloat16 [8192, 8192], P('batch', 'heads'), may hold values from -0.0625 to 0.0625
- w_emb: bfloat16 [8192, 8192], P('batch', 'heads'), may hold values from -0.0625 to 0.0625
Outputs:
- verified_hidden: bfloat16 [1280, 8192], P(None, 'batch')
- draft_feat: bfloat16 [128, 2, 5, 8192], P('batch', None, None, 'heads')
All inputs are finite; a program needn't handle non-finite values.
Results may differ from a plain program's by a relative error of at most 0.0043.
Values may be sent and summed in bfloat16 or wider, within the bound.
A program may use at most 128 MiB of HBM per device.

v0:
```python
import jax
import jax.numpy as jnp
from jax import lax
from jax.sharding import PartitionSpec as P

D = 8192
HD = 128


def attend_local(queries, new_kv, cache_kv, lengths, accepted):
    rows, _, steps, qcols = queries.shape
    slots = cache_kv.shape[2]
    kv_heads = cache_kv.shape[3] // HD
    q_heads = qcols // HD
    group = q_heads // kv_heads
    qv = queries.reshape(rows, 2, steps, kv_heads, group, HD)
    keys = jnp.concatenate(
        [
            cache_kv[:, 0].reshape(rows, slots, kv_heads, HD),
            new_kv[:, :, 0].reshape(rows, 2 * steps, kv_heads, HD),
        ],
        axis=1,
    )
    vals = jnp.concatenate(
        [
            cache_kv[:, 1].reshape(rows, slots, kv_heads, HD),
            new_kv[:, :, 1].reshape(rows, 2 * steps, kv_heads, HD),
        ],
        axis=1,
    )
    scores = jnp.einsum(
        "rtigjd,rkgd->rtigjk", qv, keys, preferred_element_type=jnp.float32
    ) / jnp.sqrt(jnp.float32(HD))
    width = slots + 2 * steps
    slot = jnp.arange(width, dtype=jnp.int32)[None, None, None, :]
    rnd = jnp.arange(2, dtype=jnp.int32)[None, :, None, None]
    pos = jnp.arange(steps, dtype=jnp.int32)[None, None, :, None]
    first = slot - slots
    second = slot - slots - steps
    seen = slot < lengths[:, None, None, None]
    seen = seen | (first >= 0) & (first < steps) & (
        (rnd == 0) & (first <= pos) | (rnd == 1) & (first <= accepted[:, None, None, None])
    )
    seen = seen | (second >= 0) & (rnd == 1) & (second <= pos)
    seen = seen[:, :, :, None, None, :]
    masked = jnp.where(seen, scores, jnp.float32(-1e30))
    top = jnp.max(masked, axis=-1, keepdims=True)
    expo = jnp.where(seen, jnp.exp(masked - top), jnp.float32(0.0))
    weights = (expo / jnp.sum(expo, axis=-1, keepdims=True)).astype(jnp.bfloat16)
    out = jnp.einsum("rtigjk,rkgd->rtigjd", weights, vals, preferred_element_type=jnp.float32)
    return out.astype(jnp.bfloat16).reshape(rows * 2 * steps, qcols)


def normalize(hidden, gain, total_squares):
    scale = lax.rsqrt(total_squares[:, None] / D + 1e-05)
    return (hidden * scale * gain[None, :]).astype(jnp.bfloat16)


def body(
    token_ids, accepted, lengths, queries, new_kv, cache_kv, table, w_out, gain, w_feat, w_emb
):
    rows, _, steps = token_ids.shape
    all_ids = lax.all_gather(token_ids.reshape(-1), "batch", axis=0, tiled=True)
    vocab_rows = table.shape[0]
    base = lax.axis_index("heads") * vocab_rows
    local_ids = all_ids - base
    inside = (local_ids >= 0) & (local_ids < vocab_rows)
    picked = jnp.take(table, jnp.clip(local_ids, 0, vocab_rows - 1), axis=0)
    partial_emb = jnp.where(inside[:, None], picked.astype(jnp.float32), jnp.float32(0.0))
    emb = lax.psum(partial_emb.astype(jnp.bfloat16), "heads").astype(jnp.float32)
    emb_bf = emb.astype(jnp.bfloat16)
    attn = attend_local(queries, new_kv, cache_kv, lengths, accepted)
    partial_proj = jnp.dot(
        lax.all_gather(attn, "batch", axis=0, tiled=True), w_out, preferred_element_type=jnp.float32
    )
    share = lax.psum_scatter(partial_proj, "heads", scatter_dimension=0, tiled=True)
    share_rows = share.shape[0]
    start = lax.axis_index("heads") * share_rows
    hidden = lax.dynamic_slice_in_dim(emb, start, share_rows, 0) + share
    total_squares = lax.psum(jnp.sum(hidden * hidden, axis=1), "batch")
    feat_share = normalize(hidden, gain, total_squares)
    hidden_bf, feat_bf = (
        lax.all_gather(hidden.astype(jnp.bfloat16), "heads", axis=0, tiled=True),
        lax.all_gather(feat_share, "heads", axis=0, tiled=True),
    )
    draft = lax.psum_scatter(
        jnp.dot(feat_bf, w_feat, preferred_element_type=jnp.float32)
        + jnp.dot(emb_bf, w_emb, preferred_element_type=jnp.float32),
        "batch",
        scatter_dimension=0,
        tiled=True,
    )
    draft = draft.astype(jnp.bfloat16).reshape(rows, 2, steps, w_feat.shape[1])
    return (hidden_bf, draft)


def solution(mesh):
    placed = (
        P("batch", None, None),
        P("batch"),
        P("batch"),
        P("batch", None, None, "heads"),
        P("batch", None, None, None, "heads"),
        P("batch", None, None, "heads"),
        P("heads", "batch"),
        P("heads", "batch"),
        P("batch"),
        P("batch", "heads"),
        P("batch", "heads"),
    )
    return jax.shard_map(
        body,
        mesh=mesh,
        in_specs=placed,
        out_specs=(P(None, "batch"), P("batch", None, None, "heads")),
        check_vma=False,
    )
```

profile of v0, /device:TPU:0, one launch (start us, length us, event | category | flops | bytes accessed | tf_op | source)
XLA Modules:
  0.0 490.2 jit_solution(2593413514648371541)
XLA Ops:
  9.9 5.7 %fusion.19 = (bf16[8,1,512,512]{3,2,1,0:T(8,128)(2,1)}, bf16[8,1,512,512]{3,2,1,0:T(8,128)(2,1)}) fusion(bf16[8,2,512,512]{3,2,1,0:T(8,128)(2,1)} %param.16), kind=kLoop, calls=%fused_computation.50 | loop fusion | bytes 16777216 | tf_op jit(solution)/shard_map/slice | solution.py:26
  15.7 6.5 %copy.32 = bf16[8,1,512,512]{2,3,0,1:T(8,128)(2,1)} copy(bf16[8,1,512,512]{3,2,1,0:T(8,128)(2,1)} %get-tuple-element.9) | data formatting | bytes 8388608
  22.1 6.5 %copy.23 = bf16[8,512,4,128]{3,1,2,0:T(8,128)(2,1)} copy(bf16[8,512,4,128]{1,3,2,0:T(8,128)(2,1)} %bitcast.40) | data formatting | bytes 8388608 | tf_op jit(solution)/shard_map/reshape;squeeze | solution.py:19
  29.2 6.5 %copy.30 = bf16[8,1,512,512]{2,3,0,1:T(8,128)(2,1)} copy(bf16[8,1,512,512]{3,2,1,0:T(8,128)(2,1)} %get-tuple-element.8) | data formatting | bytes 8388608
  35.7 6.4 %copy.19 = bf16[8,512,4,128]{3,1,2,0:T(8,128)(2,1)} copy(bf16[8,512,4,128]{1,3,2,0:T(8,128)(2,1)} %bitcast.41) | data formatting | bytes 8388608 | tf_op jit(solution)/shard_map/reshape;squeeze | solution.py:26
  42.2 3.9 fusion.4
  46.3 4.0 fusion.21
  54.6 14.2 %all-reduce = s32[1280]{0:T(1024)S(1)} all-reduce(s32[1280]{0:T(1024)S(1)} %dynamic-update-slice), channel_id=1, replica_groups=mesh['batch'=16,'heads'=2] {'batch'}, use_global_device_ids=true, to_apply=%add | all-reduce | flops 1280 | bytes 10240
  68.8 25.1 %gather_fusion = bf16[1280,512]{1,0:T(8,128)(2,1)S(1)} fusion(bf16[32768,512]{1,0:T(8,128)(2,1)} %param.17, s32[2048]{0:T(1024)S(1)} %pad_clamp_fusion), kind=kCustom, calls=%fused_computation | custom fusion | bytes 2626560 | tf_op jit(solution)/shard_map/jit(_take)/gather | solution.py:68
  93.8 1.9 select_convert_fusion
  95.8 15.8 %all-gather.4.cloned.1.call-done = bf16[1280,2048]{1,0:T(8,128)(2,1)} async-done(((bf16[80,2048]{1,0:T(8,128)(2,1)}), bf16[1280,2048]{1,0:T(8,128)(2,1)}) %all-gather.4.cloned.1.call-update) | async-done | bytes 5242896 | tf_op jit(solution)/shard_map/all_gather | solution.py:74
  111.6 6.9 %fusion.22 = f32[1280,512]{1,0:T(8,128)} fusion(bf16[1280,2048]{1,0:T(8,128)(2,1)} %all-gather.4.cloned.1.call-done, bf16[2048,512]{1,0:T(8,128)(2,1)S(1)} %copy-done), kind=kOutput, calls=%fused_computation.53 | convolution fusion | flops 2684354560 | bytes 9961472 | tf_op jit(solution)/shard_map/dot_general | solution.py:73
  118.6 20.9 %all-reduce.3.cloned.1.call-done = bf16[1280,512]{1,0:T(8,128)(2,1)} async-done(((bf16[1280,512]{1,0:T(8,128)(2,1)}), bf16[1280,512]{1,0:T(8,128)(2,1)}) %all-reduce.3.cloned.1.call-update) | async-done | bytes 1310736 | tf_op jit(solution)/shard_map/psum | solution.py:70
  139.5 39.7 %reduce-scatter.3.cloned.1.call-done = f32[640,512]{1,0:T(8,128)} async-done(((f32[1280,512]{1,0:T(8,128)}), f32[640,512]{1,0:T(8,128)}) %reduce-scatter.3.cloned.1.call-update) | async-done | bytes 1310736 | tf_op jit(solution)/shard_map/reduce_scatter | solution.py:76
  179.2 1.7 multiply_reduce_fusion
  181.0 33.1 %psum.15 = f32[640]{0:T(1024)S(1)} all-reduce(f32[640]{0:T(1024)S(1)} %multiply_reduce_fusion), channel_id=1, replica_groups=mesh['batch'=16,'heads'=2] {'batch'}, use_global_device_ids=true, to_apply=%region_5.6 | all-reduce | flops 640 | bytes 5120 | tf_op jit(solution)/shard_map/psum | solution.py:80
  214.0 2.8 multiply_convert_fusion
  217.8 19.5 %all-gather.8.cloned.1.call-done = bf16[1280,512]{1,0:T(8,128)(2,1)} async-done(((bf16[640,512]{1,0:T(8,128)(2,1)}), bf16[1280,512]{1,0:T(8,128)(2,1)}) %all-gather.8.cloned.1.call-update) | async-done | bytes 1310736 | tf_op jit(solution)/shard_map/all_gather | solution.py:84
  237.4 12.7 %fusion.23 = f32[1280,4096]{1,0:T(8,128)} fusion(bf16[1280,512]{1,0:T(8,128)(2,1)} %all-gather.8.cloned.1.call-done, bf16[512,4096]{1,0:T(8,128)(2,1)} %param.20), kind=kOutput, calls=%fused_computation.54 | convolution fusion | flops 5368709120 | bytes 26476544 | tf_op jit(solution)/shard_map/dot_general | solution.py:87
  250.1 13.9 %convolution_add_fusion = f32[1280,4096]{1,0:T(8,128)} fusion(f32[1280,4096]{1,0:T(8,128)} %fusion.23, bf16[1280,512]{1,0:T(8,128)(2,1)S(1)} %copy-done.2, bf16[512,4096]{1,0:T(8,128)(2,1)S(1)} %copy-done.4), kind=kOutput, calls=%fused_computation.2 | convolution fusion | flops 5373952000 | bytes 47448064 | tf_op jit(solution)/shard_map/dot_general | solution.py:88
  264.1 210.9 %reduce-scatter.5.cloned.1.call-done = f32[80,4096]{1,0:T(8,128)} async-done(((f32[1280,4096]{1,0:T(8,128)}), f32[80,4096]{1,0:T(8,128)}) %reduce-scatter.5.cloned.1.call-update) | async-done | bytes 1310736 | tf_op jit(solution)/shard_map/reduce_scatter | solution.py:86
  475.0 2.2 convert_element_type.36
  478.6 1.6 copy.27
  480.2 2.5 copy.39
  (65 shorter events, 8.6 us)
Async XLA Ops:
  8.0 103.6 %copy-start = (bf16[2048,512]{1,0:T(8,128)(2,1)S(1)}, bf16[2048,512]{1,0:T(8,128)(2,1)}, u32[]{:S(2)}) copy-start(bf16[2048,512]{1,0:T(8,128)(2,1)} %param.18) | copy-start | bytes 6291460
  8.0 103.6 %all-gather.4.cloned.1.call-start = ((), (), s32[]{:S(2)}) async-start(), calls=%async_computation.3 | async-start | bytes 5570560 | tf_op jit(solution)/shard_map/all_gather | solution.py:74
  22.1 6.6 %copy-start.5 = (bf16[8,2,2,5,512]{4,2,3,1,0:T(2,128)(2,1)S(1)}, bf16[8,2,2,5,512]{4,2,3,1,0:T(2,128)(2,1)}, u32[]{:S(2)}) copy-start(bf16[8,2,2,5,512]{4,2,3,1,0:T(2,128)(2,1)} %param.15) | copy-start | bytes 491524
  22.1 6.9 %copy-start.6 = (bf16[8,2,5,2048]{3,1,2,0:T(2,128)(2,1)S(1)}, bf16[8,2,5,2048]{3,1,2,0:T(2,128)(2,1)}, u32[]{:S(2)}) copy-start(bf16[8,2,5,2048]{3,1,2,0:T(2,128)(2,1)} %param.14) | copy-start | bytes 983044
  46.3 4.0 copy-start.3
  50.3 2.5 copy-start.7
  50.4 2.7 copy-start.9
  52.8 86.8 %all-reduce.3.cloned.1.call-start = ((), (), s32[]{:S(2)}) async-start(), calls=%async_computation.2 | async-start | bytes 2621440 | tf_op jit(solution)/shard_map/psum | solution.py:70
  95.7 83.5 %reduce-scatter.3.cloned.1.call-start = ((), (), s32[]{:S(2)}) async-start(), calls=%async_computation.4 | async-start | bytes 3932160 | tf_op jit(solution)/shard_map/reduce_scatter | solution.py:76
  118.5 95.5 %copy-start.8 = (f32[512]{0:T(512)S(1)}, f32[512]{0:T(512)}, u32[]{:S(2)}) copy-start(f32[512]{0:T(512)} %param.19) | copy-start | bytes 6148
  118.6 118.8 %all-gather.8.cloned.1.call-start = ((), (), s32[]{:S(2)}) async-start(), calls=%async_computation.6 | async-start | bytes 1966080 | tf_op jit(solution)/shard_map/all_gather | solution.py:84
  216.8 47.3 %all-gather.6.cloned.1.call-start = ((), (), s32[]{:S(2)}) async-start(), calls=%async_computation.5 | async-start | bytes 1966080 | tf_op jit(solution)/shard_map/all_gather | solution.py:83
  217.6 32.5 %copy-start.2 = (bf16[1280,512]{1,0:T(8,128)(2,1)S(1)}, bf16[1280,512]{1,0:T(8,128)(2,1)}, u32[]{:S(2)}) copy-start(bf16[1280,512]{1,0:T(8,128)(2,1)} %all-reduce.3.cloned.1.call-done) | copy-start | bytes 3932164
  217.6 257.4 %reduce-scatter.5.cloned.1.call-start = ((), (), s32[]{:S(2)}) async-start(), calls=%async_computation.7 | async-start | bytes 22282240 | tf_op jit(solution)/shard_map/reduce_scatter | solution.py:86
  237.4 12.7 %copy-start.4 = (bf16[512,4096]{1,0:T(8,128)(2,1)S(1)}, bf16[512,4096]{1,0:T(8,128)(2,1)}, u32[]{:S(2)}) copy-start(bf16[512,4096]{1,0:T(8,128)(2,1)} %param.21) | copy-start | bytes 12582916
  264.1 218.6 %copy-start.1 = (bf16[2048,512]{1,0:T(8,128)(2,1)S(1)}, bf16[2048,512]{1,0:T(8,128)(2,1)}, u32[]{:S(2)}) copy-start(bf16[2048,512]{1,0:T(8,128)(2,1)} %param.18) | copy-start | bytes 6291460
Sparse Core Ops, SparseCore 0:
  52.9 58.6 all-gather.3
  264.2 210.8 reduce-scatter.4
Sparse Core Ops, SparseCore 1:
  95.8 43.6 all-reduce.2
  141.7 37.5 reduce-scatter.2
  216.9 20.4 all-gather.7
  239.5 24.1 all-gather.5
where the time goes:
time: 491 us; the launch traced here: 490 us
  waiting for transfers between devices  308 us (63%)
  local copies, waits for them, and re-layouts  64.9 us (13%)
  blocking collectives  47.3 us (10%)
  matrix products  38.8 us (8%)
  between operations  16.6 us (3%)
  other arithmetic  14.6 us (3%)
    reduce_scatter x1, waiting for transfers between devices, body(): lax.psum_scatter(jnp.dot(feat_bf, w_feat, preferred_element_type=jnp.floa...  211 us
    reduce_scatter x1, waiting for transfers between devices, body(): lax.psum_scatter(partial_proj, 'heads', scatter_dimension=0, tiled=True)  39.7 us
    psum x1, blocking collectives, body(): total_squares = lax.psum(jnp.sum(hidden * hidden, axis=1), 'batch')  33.1 us
    gather x1, local copies, waits for them, and re-layouts, body(): picked = jnp.take(table, jnp.clip(local_ids, 0, vocab_rows - 1), axis=0)  25.1 us
    psum x1, waiting for transfers between devices, body(): lax.psum(partial_emb.astype(jnp.bfloat16), 'heads').astype(jnp.float32)  20.9 us
    all_gather x1, waiting for transfers between devices, body(): lax.all_gather(feat_share, 'heads', axis=0, tiled=True)  19.5 us
    unnamed x30, local copies, waits for them, and re-layouts  18.1 us
    all_gather x1, waiting for transfers between devices, body(): lax.all_gather(attn, 'batch', axis=0, tiled=True)  15.8 us
  transfers between devices with their start and end apart: 6, of which 5 were waited for; matrix products, arithmetic and copies ran while one was open for 13% of the time, Pallas kernels for 0%

commit v1 on v0

v1 whole, which is shorter than its diff:
```python
import functools

import jax
import jax.numpy as jnp
from jax import lax
from jax.experimental import pallas as pl
from jax.experimental.pallas import tpu as pltpu
from jax.sharding import PartitionSpec as P

HD = 128
MESH = pl.DeviceIdType.MESH
VMEM_LIMIT = 60 * 1024 * 1024


def attend_kernel(steps, group, kv_heads, len_ref, acc_ref, q_ref, kv_ref, new_ref, out_ref):
    row = pl.program_id(0)
    length = len_ref[row]
    accepted = acc_ref[row]
    queries = q_ref.shape[2]
    slots = kv_ref.shape[2]
    fresh = new_ref.shape[2]
    shape = (queries, fresh)
    at = lax.broadcasted_iota(jnp.int32, shape, 0)
    new = lax.broadcasted_iota(jnp.int32, shape, 1)
    rnd = at // (steps * group)
    pos = (at // group) % steps
    seen_new = (new < steps) & (
        ((rnd == 0) & (new <= pos)) | ((rnd == 1) & (new <= accepted))
    )
    seen_new = seen_new | (
        (new >= steps) & (new < 2 * steps) & (rnd == 1) & (new - steps <= pos)
    )
    seen = lax.broadcasted_iota(jnp.int32, (queries, slots), 1) < length
    root = jnp.sqrt(jnp.float32(HD))
    low = jnp.float32(-1e30)
    rows_dot = (((1,), (1,)), ((), ()))
    for j in range(kv_heads):
        cols = slice(j * HD, (j + 1) * HD)
        q = q_ref[0, j]
        s = lax.dot_general(q, kv_ref[0, 0, :, cols], rows_dot, preferred_element_type=jnp.float32)
        sn = lax.dot_general(q, new_ref[0, 0, :, cols], rows_dot, preferred_element_type=jnp.float32)
        s = jnp.where(seen, s / root, low)
        sn = jnp.where(seen_new, sn / root, low)
        top = jnp.maximum(jnp.max(s, axis=1, keepdims=True), jnp.max(sn, axis=1, keepdims=True))
        e = jnp.where(seen, jnp.exp(s - top), 0.0)
        en = jnp.where(seen_new, jnp.exp(sn - top), 0.0)
        total = jnp.sum(e, axis=1, keepdims=True) + jnp.sum(en, axis=1, keepdims=True)
        w = (e / total).astype(jnp.bfloat16)
        wn = (en / total).astype(jnp.bfloat16)
        out = jnp.dot(w, kv_ref[0, 1, :, cols], preferred_element_type=jnp.float32)
        out = out + jnp.dot(wn, new_ref[0, 1, :, cols], preferred_element_type=jnp.float32)
        out_ref[0, j] = out.astype(jnp.bfloat16)


def attend_local(queries, new_kv, cache_kv, lengths, accepted):
    rows, _, steps, qcols = queries.shape
    slots, cols = cache_kv.shape[2:]
    kv_heads = cols // HD
    group = qcols // cols
    count = 2 * steps * group
    q = queries.reshape(rows, 2 * steps, kv_heads, group, HD)
    q = q.transpose(0, 2, 1, 3, 4).reshape(rows, kv_heads, count, HD)
    fresh = -(-2 * steps // 16) * 16
    new = new_kv.transpose(0, 2, 1, 3, 4).reshape(rows, 2, 2 * steps, cols)
    new = jnp.pad(new, ((0, 0), (0, 0), (0, fresh - 2 * steps), (0, 0)))
    out = pl.pallas_call(
        functools.partial(attend_kernel, steps, group, kv_heads),
        grid_spec=pltpu.PrefetchScalarGridSpec(
            num_scalar_prefetch=2,
            grid=(rows,),
            in_specs=[
                pl.BlockSpec((1, kv_heads, count, HD), lambda r, a, b: (r, 0, 0, 0)),
                pl.BlockSpec((1, 2, slots, cols), lambda r, a, b: (r, 0, 0, 0)),
                pl.BlockSpec((1, 2, fresh, cols), lambda r, a, b: (r, 0, 0, 0)),
            ],
            out_specs=pl.BlockSpec((1, kv_heads, count, HD), lambda r, a, b: (r, 0, 0, 0)),
        ),
        out_shape=jax.ShapeDtypeStruct((rows, kv_heads, count, HD), jnp.bfloat16),
        compiler_params=pltpu.CompilerParams(vmem_limit_bytes=VMEM_LIMIT),
        cost_estimate=pl.CostEstimate(
            flops=4 * rows * kv_heads * count * slots * HD,
            bytes_accessed=2 * cache_kv.size,
            transcendentals=rows * kv_heads * count * slots,
        ),
    )(lengths, accepted, q, cache_kv, new)
    out = out.reshape(rows, kv_heads, 2 * steps, group, HD).transpose(0, 2, 1, 3, 4)
    return out.reshape(rows * 2 * steps, qcols)


def splits(n):
    cores = 2 if n % 2 == 0 else 1
    ys = 2 if n % (2 * cores) == 0 else 1
    return cores, ys, n // (cores * ys)


def draft_kernel(
    n, width, chunks, depth_all,
    own_ref, other_ref, emb_ref, gain_ref, wf_ref, we_ref, out_ref,
    x, sq, send1, recv1, own1, send2, recv2, own2, send3, recv3, own3,
    sq_send, sq_recv, s1, r1, s2, r2, s3, r3,
):
    nc, ny, nz = splits(n)
    me = lax.axis_index("batch")
    core = me % nc
    y = (me // nc) % ny
    z = me // (nc * ny)
    share = out_ref.shape[0]
    depth = own_ref.shape[1]
    groups = nz * ny

    def hidden_of(owner):
        at = pl.ds(owner * share, share)
        proj = own_ref[at, :].astype(jnp.float32) + other_ref[at, :].astype(jnp.float32)
        return emb_ref[at, :].astype(jnp.float32) + proj

    barrier = pltpu.get_barrier_semaphore()
    for d in range(1, n):
        pl.semaphore_signal(
            barrier, inc=1, device_id={"batch": (me + d) % n}, device_id_type=MESH
        )

    ones = jnp.ones((8, depth), jnp.float32)
    everything = own_ref[...].astype(jnp.float32) + other_ref[...].astype(jnp.float32)
    everything = emb_ref[...].astype(jnp.float32) + everything
    squares = lax.dot_general(
        ones, everything * everything, (((1,), (1,)), ((), ())),
        preferred_element_type=jnp.float32, precision=lax.Precision.HIGHEST,
    )
    sq[me] = squares[:1]
    pl.semaphore_wait(barrier, n - 1)

    copies = []
    for d in range(1, n):
        copy = pltpu.make_async_remote_copy(
            src_ref=sq.at[me], dst_ref=sq.at[me],
            send_sem=sq_send.at[d], recv_sem=sq_recv.at[d],
            device_id={"batch": (me + d) % n}, device_id_type=MESH,
        )
        copy.start()
        copies.append(copy)
    for copy in copies:
        copy.wait()

    total = sq[0]
    for d in range(1, n):
        total = total + sq[d]
    total = jnp.broadcast_to(total, (8, total.shape[1]))
    scale = lax.rsqrt(total / depth_all + 1e-05)
    column = jnp.transpose(scale)[:, :1]
    for owner in range(n):
        at = slice(owner * share, (owner + 1) * share)
        place = slice((owner // nc) * share, (owner // nc + 1) * share)
        feat = hidden_of(owner) * column[at] * gain_ref[...]
        x[owner % nc, place, :depth] = feat.astype(jnp.bfloat16)
        x[owner % nc, place, depth:] = emb_ref[at, :]

    def product(t, which):
        cols = pl.ds(pl.multiple_of(t * width, width), width)
        rows = x[which]
        out = jnp.dot(rows[:, :depth], wf_ref[:, cols], preferred_element_type=jnp.float32)
        return out + jnp.dot(rows[:, depth:], we_ref[:, cols], preferred_element_type=jnp.float32)

    def core_copy(t):
        return pltpu.make_async_remote_copy(
            src_ref=send1.at[t], dst_ref=recv1.at[t], send_sem=s1.at[t], recv_sem=r1.at[t],
            device_id={"batch": me + 1 - 2 * core}, device_id_type=MESH,
        )

    def y_copy(t):
        return pltpu.make_async_remote_copy(
            src_ref=send2.at[t], dst_ref=recv2.at[t], send_sem=s2.at[t], recv_sem=r2.at[t],
            device_id={"batch": me + nc * (1 - 2 * y)}, device_id_type=MESH,
        )

    def z_copy(t, d):
        to = (z + d) % nz
        return pltpu.make_async_remote_copy(
            src_ref=send3.at[t, to], dst_ref=recv3.at[t, d], send_sem=s3.at[t, d],
            recv_sem=r3.at[t, d],
            device_id={"batch": to * (nc * ny) + me % (nc * ny)}, device_id_type=MESH,
        )

    def stage_product(t):
        if nc > 1:
            send1[t] = product(t, 1 - core).astype(jnp.bfloat16).reshape(groups, share, width)
            core_copy(t).start()
        own1[t % 2] = product(t, core).reshape(groups, share, width)

    def stage_core(t):
        if nc > 1:
            core_copy(t).wait()
        for k in range(nz):
            for v in ([1, 0] if ny > 1 else [0]):
                which = (y + v) % ny
                g = k * ny + which
                value = own1[t % 2, g]
                if nc > 1:
                    value = value + recv1[t, g].astype(jnp.float32)
                if v:
                    send2[t, k] = value.astype(jnp.bfloat16)
                else:
                    own2[t % 2, k] = value
        if ny > 1:
            y_copy(t).start()

    def stage_y(t):
        if ny > 1:
            y_copy(t).wait()
        for d in range(nz):
            to = (z + d) % nz
            value = own2[t % 2, to]
            if ny > 1:
                value = value + recv2[t, to].astype(jnp.float32)
            if d:
                send3[t, to] = value.astype(jnp.bfloat16)
                z_copy(t, d).start()
            else:
                own3[t % 2] = value

    def stage_z(t):
        value = own3[t % 2]
        for d in range(1, nz):
            z_copy(t, d).wait()
            value = value + recv3[t, d].astype(jnp.float32)
        cols = pl.ds(pl.multiple_of(t * width, width), width)
        out_ref[:, cols] = value.astype(out_ref.dtype)

    def step(t, carry):
        @pl.when(t < chunks)
        def _():
            stage_product(t)

        @pl.when((t >= 1) & (t < chunks + 1))
        def _():
            stage_core(t - 1)

        @pl.when((t >= 2) & (t < chunks + 2))
        def _():
            stage_y(t - 2)

        @pl.when(t >= 3)
        def _():
            stage_z(t - 3)

        return carry

    lax.fori_loop(0, chunks + 3, step, 0)


def draft_local(own, other, emb, gain, w_feat, w_emb, n):
    total_rows, depth = own.shape
    out_cols = w_feat.shape[1]
    share = total_rows // n
    nc, ny, nz = splits(n)
    width = 512
    while out_cols % width:
        width //= 2
    chunks = out_cols // width
    groups = ny * nz
    bf, f32 = jnp.bfloat16, jnp.float32
    dma = pltpu.SemaphoreType.DMA
    vmem = pl.BlockSpec(memory_space=pltpu.VMEM)
    return pl.pallas_call(
        functools.partial(draft_kernel, n, width, chunks, depth * n),
        out_shape=jax.ShapeDtypeStruct((share, out_cols), bf),
        in_specs=[vmem] * 6,
        out_specs=vmem,
        scratch_shapes=[
            pltpu.VMEM((nc, total_rows // nc, 2 * depth), bf),
            pltpu.VMEM((n, 1, total_rows), f32),
            pltpu.VMEM((chunks, groups, share, width), bf),
            pltpu.VMEM((chunks, groups, share, width), bf),
            pltpu.VMEM((2, groups, share, width), f32),
            pltpu.VMEM((chunks, nz, share, width), bf),
            pltpu.VMEM((chunks, nz, share, width), bf),
            pltpu.VMEM((2, nz, share, width), f32),
            pltpu.VMEM((chunks, nz, share, width), bf),
            pltpu.VMEM((chunks, nz, share, width), bf),
            pltpu.VMEM((2, share, width), f32),
            dma((n,)),
            dma((n,)),
            dma((chunks,)),
            dma((chunks,)),
            dma((chunks,)),
            dma((chunks,)),
            dma((chunks, nz)),
            dma((chunks, nz)),
        ],
        compiler_params=pltpu.CompilerParams(
            collective_id=0, has_side_effects=True, vmem_limit_bytes=VMEM_LIMIT
        ),
        cost_estimate=pl.CostEstimate(
            flops=4 * total_rows * depth * out_cols,
            bytes_accessed=4 * depth * out_cols,
            transcendentals=0,
        ),
    )(own, other, emb, gain.reshape(1, depth), w_feat, w_emb)


def swap(value):
    return lax.ppermute(value, "heads", [(0, 1), (1, 0)])


def body(
    n, nh,
    token_ids, accepted, lengths, queries, new_kv, cache_kv, table, w_out, gain, w_feat, w_emb
):
    rows, _, steps = token_ids.shape
    all_ids = lax.all_gather(token_ids.reshape(-1), "batch", axis=0, tiled=True)
    vocab_rows = table.shape[0]
    base = lax.axis_index("heads") * vocab_rows
    local_ids = all_ids - base
    inside = (local_ids >= 0) & (local_ids < vocab_rows)
    picked = jnp.take(table, jnp.clip(local_ids, 0, vocab_rows - 1), axis=0)
    partial_emb = jnp.where(inside[:, None], picked, jnp.bfloat16(0.0))
    if nh == 2:
        emb = jnp.where(inside[:, None], picked, swap(partial_emb))
    else:
        emb = lax.psum(partial_emb, "heads")
    attn = attend_local(queries, new_kv, cache_kv, lengths, accepted)
    proj = jnp.dot(
        lax.all_gather(attn, "batch", axis=0, tiled=True), w_out, preferred_element_type=jnp.float32
    )
    if nh == 2:
        own = proj.astype(jnp.bfloat16)
        other = swap(own)
    else:
        proj = lax.psum(proj, "heads")
        own = proj.astype(jnp.bfloat16)
        other = (proj - own.astype(jnp.float32)).astype(jnp.bfloat16)
    hidden = emb.astype(jnp.float32) + (own.astype(jnp.float32) + other.astype(jnp.float32))
    draft = draft_local(own, other, emb, gain, w_feat, w_emb, n)
    return (hidden.astype(jnp.bfloat16), draft.reshape(rows, 2, steps, w_feat.shape[1]))


def solution(mesh):
    placed = (
        P("batch", None, None),
        P("batch"),
        P("batch"),
        P("batch", None, None, "heads"),
        P("batch", None, None, None, "heads"),
        P("batch", None, None, "heads"),
        P("heads", "batch"),
        P("heads", "batch"),
        P("batch"),
        P("batch", "heads"),
        P("batch", "heads"),
    )
    return jax.shard_map(
        functools.partial(body, mesh.shape["batch"], mesh.shape["heads"]),
        mesh=mesh,
        in_specs=placed,
        out_specs=(P(None, "batch"), P("batch", None, None, "heads")),
        check_vma=False,
    )
```

time: 491 us -> 226 us (0.46)
  waiting for transfers between devices: 308 us -> 47.5 us
  Pallas kernels: 0 us -> 99.1 us
  matrix products: 38.8 us -> 5.36 us
  blocking collectives: 47.3 us -> 14.2 us
  local copies, waits for them, and re-layouts: 64.9 us -> 34.3 us
  other arithmetic: 14.6 us -> 5.81 us
    reduce_scatter x2 -> x0, waiting for transfers between devices: 251 us -> none  [the longest x1 211 us: body(): lax.psum_scatter(jnp.dot(feat_bf, w_feat, preferred_element_type=jnp.floa...]
    pallas_call x0 -> x2, Pallas kernels: none -> 99.1 us  [the longest x1 83.6 us: draft_local(): pl.pallas_call(functools.partial(draft_kernel, n, width, chunks, depth *...]
    ppermute x0 -> x2, waiting for transfers between devices: none -> 34.3 us  [swap(): return lax.ppermute(value, 'heads', [(0, 1), (1, 0)])]
    psum x1 -> x0, blocking collectives: 33.1 us -> none  [body(): total_squares = lax.psum(jnp.sum(hidden * hidden, axis=1), 'batch')]
    dot_general x4 -> x0, matrix products: 31.8 us -> none  [the longest x1 13.9 us: body(): jnp.dot(emb_bf, w_emb, preferred_element_type=jnp.float32)]
    psum x1 -> x0, waiting for transfers between devices: 20.9 us -> none  [body(): lax.psum(partial_emb.astype(jnp.bfloat16), 'heads').astype(jnp.float32)]
    all_gather x2 -> x0, waiting for transfers between devices: 19.6 us -> none  [the longest x1 19.5 us: body(): lax.all_gather(feat_share, 'heads', axis=0, tiled=True)]
    unnamed x30 -> x19, local copies, waits for them, and re-layouts: 18.1 us -> 4.74 us
  transfers between devices with their start and end apart: 6 -> 3, of which waited for: 5 -> 3; matrix products, arithmetic and copies ran while one was open for 13% -> 14% of each run, Pallas kernels for 0% -> 0%
where the time goes in v1:
time: 226 us
  Pallas kernels  99.1 us (44%)
  waiting for transfers between devices  47.5 us (21%)
  local copies, waits for them, and re-layouts  34.3 us (15%)
  between operations  14.8 us (7%)
  blocking collectives  14.2 us (6%)
  other arithmetic  5.81 us (3%)
  matrix products  5.36 us (2%)
  starting transfers between devices  5.06 us (2%)
    pallas_call x1, Pallas kernels, draft_local(): pl.pallas_call(functools.partial(draft_kernel, n, width, chunks, depth *...  83.6 us
    ppermute x2, waiting for transfers between devices, swap(): return lax.ppermute(value, 'heads', [(0, 1), (1, 0)])  34.3 us
    gather x1, local copies, waits for them, and re-layouts, body(): picked = jnp.take(table, jnp.clip(local_ids, 0, vocab_rows - 1), axis=0)  24.4 us
    pallas_call x1, Pallas kernels, attend_local(): pl.pallas_call(functools.partial(attend_kernel, steps, group, kv_heads),...  15.5 us
    unnamed x1, blocking collectives  14.2 us
    all_gather x1, waiting for transfers between devices, body(): lax.all_gather(attn, 'batch', axis=0, tiled=True)  13.1 us
    dot_general x1, matrix products, body(): jnp.dot(lax.all_gather(attn, 'batch', axis=0, tiled=True), w_out, preferr...  5.36 us
    ppermute x2, starting transfers between devices, swap(): return lax.ppermute(value, 'heads', [(0, 1), (1, 0)])  5.02 us
  transfers between devices with their start and end apart: 3, of which 3 were waited for; matrix products, arithmetic and copies ran while one was open for 14% of the time, Pallas kernels for 0%

profile of v1, /device:TPU:0, one launch (start us, length us, event | category | flops | bytes accessed | tf_op | source)
XLA Modules:
  0.0 226.1 jit_solution(17008961971024924773)
XLA Ops:
  7.2 1.1 copy.19
  8.4 1.1 copy.17
  9.5 0.9 copy.18
  10.3 0.7 pad.4.new_ref
  11.1 15.5 %shard_map.122 = bf16[8,4,40,128]{3,2,1,0:T(8,128)(2,1)} custom-call(s32[8]{0:T(128)} %len_ref.1, s32[8]{0:T(128)} %acc_ref.1, bf16[8,4,40,128]{3,2,1,0:T(8,128)(2,1)} %bitcast.15, bf16[8,2,512,512]{3,2,1,0:T(8,128)(2,1)} %kv_ref.1, bf16[8,2,16,512]{3,2,1,0:T(8,128)(2,1)} %pad.4.new_ref), custom_call_target="tpu_custom_call" | custom-call | flops 335544320 | bytes 8388608 | tf_op jit(solution)/shard_map/pallas_call | solution.py:66
  26.5 1.1 copy.24
  27.7 1.0 reshape.39
  28.7 0.1 copy.16
  28.8 0.1 reshape.51
  28.9 0.6 dynamic-slice
  30.1 0.3 dynamic-update-slice
  30.4 14.2 %all-reduce.1 = s32[1280]{0:T(1024)S(1)} all-reduce(s32[1280]{0:T(1024)S(1)} %dynamic-update-slice), channel_id=1, replica_groups=mesh['batch'=16,'heads'=2] {'batch'}, use_global_device_ids=true, to_apply=%add.1 | all-reduce | flops 1280 | bytes 10240
  44.6 24.4 %gather_fusion = bf16[1280,512]{1,0:T(8,128)(2,1)S(1)} fusion(bf16[32768,512]{1,0:T(8,128)(2,1)} %param.17, s32[2048]{0:T(1024)S(1)} %pad_clamp_fusion), kind=kCustom, calls=%fused_computation | custom fusion | bytes 2626560 | tf_op jit(solution)/shard_map/jit(_take)/gather | solution.py:314
  69.1 1.8 broadcast_select_fusion.2
  70.9 3.5 %collective-permute-start = (bf16[1280,512]{1,0:T(8,128)(2,1)}, bf16[1280,512]{1,0:T(8,128)(2,1)}, u32[]{:S(2)}, u32[]{:S(2)}) collective-permute-start(bf16[1280,512]{1,0:T(8,128)(2,1)} %broadcast_select_fusion.2), channel_id=1, source_target_pairs={{0,1},{1,0},{2,3},{3,2},{4,5},{5,4},{6,7},{7,6},{8,9},{9,8},{10,11... | collective-permute-start | bytes 3932168 | tf_op jit(solution)/shard_map/ppermute | solution.py:301
  74.4 13.1 %all-gather.2.cloned.1.call-done = bf16[1280,2048]{1,0:T(8,128)(2,1)} async-done(((bf16[80,2048]{1,0:T(8,128)(2,1)}), bf16[1280,2048]{1,0:T(8,128)(2,1)}) %all-gather.2.cloned.1.call-update) | async-done | bytes 5242896 | tf_op jit(solution)/shard_map/all_gather | solution.py:322
  87.5 5.4 %convolution_convert_fusion.own_ref = bf16[1280,512]{1,0:T(8,128)(2,1)S(1)} fusion(bf16[1280,2048]{1,0:T(8,128)(2,1)} %all-gather.2.cloned.1.call-done, bf16[2048,512]{1,0:T(8,128)(2,1)S(1)} %copy-done), kind=kOutput, calls=%fused_computation.1 | convolution fusion | flops 2685009920 | bytes 8650752 | tf_op jit(solution)/shard_map/dot_general | solution.py:321
  92.9 1.5 collective-permute-start.1
  94.4 10.0 %collective-permute-done = bf16[1280,512]{1,0:T(8,128)(2,1)} collective-permute-done((bf16[1280,512]{1,0:T(8,128)(2,1)}, bf16[1280,512]{1,0:T(8,128)(2,1)}, u32[]{:S(2)}, u32[]{:S(2)}) %collective-permute-start) | collective-permute-done | bytes 1310752 | tf_op jit(solution)/shard_map/ppermute | solution.py:301
  104.4 24.4 %collective-permute-done.1.other_ref = bf16[1280,512]{1,0:T(8,128)(2,1)S(1)} collective-permute-done((bf16[1280,512]{1,0:T(8,128)(2,1)S(1)}, bf16[1280,512]{1,0:T(8,128)(2,1)S(1)}, u32[]{:S(2)}, u32[]{:S(2)}) %collective-permute-start.1) | collective-permute-done | bytes 1310752 | tf_op jit(solution)/shard_map/ppermute | solution.py:301
  128.7 4.0 %add_convert_fusion = (bf16[1280,512]{1,0:T(8,128)(2,1)}, bf16[1280,512]{1,0:T(8,128)(2,1)}) fusion(bf16[1280,512]{1,0:T(8,128)(2,1)S(1)} %collective-permute-done.1.other_ref, bf16[1280,512]{1,0:T(8,128)(2,1)S(1)} %convolution_convert_fusion.own_ref, bf16[1280,512]{1,0:T(8,128)(2,1)} %collective-permute-done, bf16[1280,512]{1,0:T(8,128)(2,1)S(1)} %gather_fusion, ...), kind=kLoop, calls=%fused_computation.2 | loop fusion | flops 5242880 | bytes 7866880 | tf_op jit(solution)/shard_map/convert_element_type | solution.py:333
  132.7 83.6 %shard_map.123 = bf16[80,4096]{1,0:T(8,128)(2,1)} custom-call(bf16[1280,512]{1,0:T(8,128)(2,1)} %copy-done.2, bf16[1280,512]{1,0:T(8,128)(2,1)} %copy-done.3, bf16[1280,512]{1,0:T(8,128)(2,1)} %get-tuple-element.7.emb_ref, f32[1,512]{1,0:T(1,128)} %bitcast.20, bf16[512,4096]{1,0:T(8,128)(2,1)} %wf_ref.1, bf16[512,4096]{1,0:T(8,128)(2,1)} %we_ref.1), custom_call_target="tpu_custom_call" | custom-call | flops 10737418240 | bytes 8388608 | tf_op jit(solution)/shard_map/pallas_call | solution.py:263
  216.4 1.4 reshape.41
  217.7 1.6 copy.22
  (18 shorter events, 0.2 us)
Async XLA Ops:
  7.2 80.3 %copy-start = (bf16[2048,512]{1,0:T(8,128)(2,1)S(1)}, bf16[2048,512]{1,0:T(8,128)(2,1)}, u32[]{:S(2)}) copy-start(bf16[2048,512]{1,0:T(8,128)(2,1)} %param.18) | copy-start | bytes 6291460
  7.2 80.3 %all-gather.2.cloned.1.call-start = ((), (), s32[]{:S(2)}) async-start(), calls=%async_computation | async-start | bytes 5570560 | tf_op jit(solution)/shard_map/all_gather | solution.py:322
  26.5 2.1 copy-start.4
  26.5 2.3 %copy-start.5 = (u32[32]{0:T(128)S(1)}, u32[32]{0:T(128)}, u32[]{:S(2)}) copy-start(u32[32]{0:T(128)} %constant.38) | copy-start | bytes 388
  70.9 33.5 %collective-permute-start = (bf16[1280,512]{1,0:T(8,128)(2,1)}, bf16[1280,512]{1,0:T(8,128)(2,1)}, u32[]{:S(2)}, u32[]{:S(2)}) collective-permute-start(bf16[1280,512]{1,0:T(8,128)(2,1)} %broadcast_select_fusion.2), channel_id=1, source_target_pairs={{0,1},{1,0},{2,3},{3,2},{4,5},{5,4},{6,7},{7,6},{8,9},{9,8},{10,11... | collective-permute-start | bytes 3932168 | tf_op jit(solution)/shard_map/ppermute | solution.py:301
  92.9 39.9 %copy-start.2 = (bf16[1280,512]{1,0:T(8,128)(2,1)}, bf16[1280,512]{1,0:T(8,128)(2,1)S(1)}, u32[]{:S(2)}) copy-start(bf16[1280,512]{1,0:T(8,128)(2,1)S(1)} %convolution_convert_fusion.own_ref) | copy-start | bytes 3932164
  92.9 35.9 %collective-permute-start.1 = (bf16[1280,512]{1,0:T(8,128)(2,1)S(1)}, bf16[1280,512]{1,0:T(8,128)(2,1)S(1)}, u32[]{:S(2)}, u32[]{:S(2)}) collective-permute-start(bf16[1280,512]{1,0:T(8,128)(2,1)S(1)} %convolution_convert_fusion.own_ref), channel_id=1, source_target_pairs={{0,1},{1,0},{2,3},{3,2},{4,5},{5,4},{6,7},{7,6},{8,9},{9,8},{10,11... | collective-permute-start | bytes 3932168 | tf_op jit(solution)/shard_map/ppermute | solution.py:301
  128.7 4.0 %copy-start.3 = (bf16[1280,512]{1,0:T(8,128)(2,1)}, bf16[1280,512]{1,0:T(8,128)(2,1)S(1)}, u32[]{:S(2)}) copy-start(bf16[1280,512]{1,0:T(8,128)(2,1)S(1)} %collective-permute-done.1.other_ref) | copy-start | bytes 3932164
  132.7 86.6 %copy-start.1 = (bf16[2048,512]{1,0:T(8,128)(2,1)S(1)}, bf16[2048,512]{1,0:T(8,128)(2,1)}, u32[]{:S(2)}) copy-start(bf16[2048,512]{1,0:T(8,128)(2,1)} %param.18) | copy-start | bytes 6291460
Sparse Core Ops, SparseCore 0:
  28.8 58.6 all-gather.1

commit v2 on v1

--- a/solution.py
+++ b/solution.py
@@ -93,9 +93,169 @@
     return cores, ys, n // (cores * ys)
 
 
-def draft_kernel(
+def gather_project(
+    n, attn_ref, emb1_ref, emb2_ref, wo_ref, own, other, emb, landed, gat,
+    zs, zr, ys, yr, cs, cr, xs, xr, es, er,
+):
+    nc, ny, nz = splits(n)
+    me = lax.axis_index("batch")
+    head = lax.axis_index("heads")
+    core = me % nc
+    y = (me // nc) % ny
+    z = me // (nc * ny)
+    group = nc * ny
+    rows = attn_ref.shape[0] * group
+    sign = 1 - 2 * ((2 * z) // nz)
+
+    emb_copy = pltpu.make_async_remote_copy(
+        src_ref=emb2_ref, dst_ref=landed, send_sem=es, recv_sem=er,
+        device_id={"heads": 1 - head}, device_id_type=MESH,
+    )
+    emb_copy.start()
+    gat[me] = attn_ref[...]
+
+    def z_copy(block, way, to):
+        at = block * group + me % group
+        return pltpu.make_async_remote_copy(
+            src_ref=gat.at[at], dst_ref=gat.at[at],
+            send_sem=zs.at[way, block], recv_sem=zr.at[way, block],
+            device_id={"batch": to * group + me % group}, device_id_type=MESH,
+        )
+
+    def y_copy(block):
+        at = block * group + me % group
+        return pltpu.make_async_remote_copy(
+            src_ref=gat.at[at], dst_ref=gat.at[at], send_sem=ys.at[block], recv_sem=yr.at[block],
+            device_id={"batch": me + nc * (1 - 2 * y)}, device_id_type=MESH,
+        )
+
+    def core_copy(block, line):
+        at = block * group + line * nc + core
+        return pltpu.make_async_remote_copy(
+            src_ref=gat.at[at], dst_ref=gat.at[at],
+            send_sem=cs.at[block, line], recv_sem=cr.at[block, line],
+            device_id={"batch": me + 1 - 2 * core}, device_id_type=MESH,
+        )
+
+    def x_copy(block):
+        at = pl.ds(pl.multiple_of(block * rows, 16), rows)
+        return pltpu.make_async_remote_copy(
+            src_ref=own.at[at], dst_ref=other.at[at], send_sem=xs.at[block], recv_sem=xr.at[block],
+            device_id={"heads": 1 - head}, device_id_type=MESH,
+        )
+
+    def spread(block):
+        if ny > 1:
+            y_copy(block).start()
+        if nc > 1:
+            core_copy(block, y).start()
+
+    def finish(i):
+        block = (z + sign * i + nz) % nz
+        if ny > 1:
+            y_copy(block).wait()
+            if nc > 1:
+                core_copy(block, 1 - y).start()
+        if nc > 1:
+            for line in range(ny):
+                core_copy(block, line).wait()
+        value = gat[pl.ds(block * group, group)].reshape(rows, gat.shape[2])
+        value = jnp.dot(value, wo_ref[...], preferred_element_type=jnp.float32)
+        own[pl.ds(pl.multiple_of(block * rows, 16), rows), :] = value.astype(own.dtype)
+        x_copy(block).start()
+
+    @pl.when(z < nz - 1)
+    def _():
+        z_copy(z, 0, z + 1).start()
+
+    @pl.when(z > 0)
+    def _():
+        z_copy(z, 1, z - 1).start()
+
+    spread(z)
+    for s in range(1, nz):
+        @pl.when(z >= s)
+        def _():
+            z_copy(z - s, 0, z).wait_recv()
+
+            @pl.when(z < nz - 1)
+            def _():
+                z_copy(z - s, 0, z + 1).start()
+
+            spread(z - s)
+
+        @pl.when(z + s < nz)
+        def _():
+            z_copy(z + s, 1, z).wait_recv()
+
+            @pl.when(z > 0)
+            def _():
+                z_copy(z + s, 1, z - 1).start()
+
+            spread(z + s)
+
+        finish(s - 1)
+    finish(nz - 1)
+
+    for s in range(nz):
+        @pl.when((z >= s) & (z < nz - 1))
+        def _():
+            z_copy(z - s, 0, z + 1).wait_send()
+
+        @pl.when((z + s < nz) & (z > 0))
+        def _():
+            z_copy(z + s, 1, z - 1).wait_send()
+
+    emb_copy.wait()
+    half = emb1_ref.shape[0]
+    emb[:half, :] = emb1_ref[...]
+    emb[half:, :] = emb2_ref[...] + landed[...]
+    for i in range(nz):
+        x_copy((z + sign * i + nz) % nz).wait()
+
+
+def greet(n, both):
+    me = lax.axis_index("batch")
+    barrier = pltpu.get_barrier_semaphore()
+    for d in range(1, n):
+        pl.semaphore_signal(
+            barrier, inc=1, device_id={"batch": (me + d) % n}, device_id_type=MESH
+        )
+    if both:
+        pl.semaphore_signal(
+            barrier, inc=1, device_id={"heads": 1 - lax.axis_index("heads")}, device_id_type=MESH
+        )
+    pl.semaphore_wait(barrier, n - 1 + both)
+
+
+def fused_kernel(n, width, chunks, depth_all, *refs):
+    attn, emb1, emb2, gain, wo, wf, we = refs[:7]
+    out, hid = refs[7:9]
+    front = refs[9:24]
+    own, other, emb = front[:3]
+    wf_in, we_in, w_sem = refs[24:27]
+    rest = refs[27:]
+    loads = [
+        pltpu.make_async_copy(wf, wf_in, w_sem.at[0]),
+        pltpu.make_async_copy(we, we_in, w_sem.at[1]),
+    ]
+    for load in loads:
+        load.start()
+    greet(n, 1)
+    gather_project(n, attn, emb1, emb2, wo, *front)
+    for load in loads:
+        load.wait()
+    draft(n, width, chunks, depth_all, own, other, emb, gain, wf_in, we_in, out, hid, *rest)
+
+
+def draft_kernel(n, width, chunks, depth_all, *refs):
+    greet(n, 0)
+    draft(n, width, chunks, depth_all, *refs)
+
+
+def draft(
     n, width, chunks, depth_all,
-    own_ref, other_ref, emb_ref, gain_ref, wf_ref, we_ref, out_ref,
+    own_ref, other_ref, emb_ref, gain_ref, wf_ref, we_ref, out_ref, hid_ref,
     x, sq, send1, recv1, own1, send2, recv2, own2, send3, recv3, own3,
     sq_send, sq_recv, s1, r1, s2, r2, s3, r3,
 ):
@@ -113,12 +273,6 @@
         proj = own_ref[at, :].astype(jnp.float32) + other_ref[at, :].astype(jnp.float32)
         return emb_ref[at, :].astype(jnp.float32) + proj
 
-    barrier = pltpu.get_barrier_semaphore()
-    for d in range(1, n):
-        pl.semaphore_signal(
-            barrier, inc=1, device_id={"batch": (me + d) % n}, device_id_type=MESH
-        )
-
     ones = jnp.ones((8, depth), jnp.float32)
     everything = own_ref[...].astype(jnp.float32) + other_ref[...].astype(jnp.float32)
     everything = emb_ref[...].astype(jnp.float32) + everything
@@ -127,7 +281,6 @@
         preferred_element_type=jnp.float32, precision=lax.Precision.HIGHEST,
     )
     sq[me] = squares[:1]
-    pl.semaphore_wait(barrier, n - 1)
 
     copies = []
     for d in range(1, n):
@@ -150,7 +303,9 @@
     for owner in range(n):
         at = slice(owner * share, (owner + 1) * share)
         place = slice((owner // nc) * share, (owner // nc + 1) * share)
-        feat = hidden_of(owner) * column[at] * gain_ref[...]
+        hidden = hidden_of(owner)
+        hid_ref[at, :] = hidden.astype(hid_ref.dtype)
+        feat = hidden * column[at] * gain_ref[...]
         x[owner % nc, place, :depth] = feat.astype(jnp.bfloat16)
         x[owner % nc, place, depth:] = emb_ref[at, :]
 
@@ -247,12 +402,13 @@
     lax.fori_loop(0, chunks + 3, step, 0)
 
 
-def draft_local(own, other, emb, gain, w_feat, w_emb, n):
-    total_rows, depth = own.shape
-    out_cols = w_feat.shape[1]
-    share = total_rows // n
+def draft_local(front, gain, w_feat, w_emb, n, w_out=None):
+    depth, out_cols = w_feat.shape
+    fused = w_out is not None
+    share = front[0].shape[0] if fused else front[0].shape[0] // n
+    total_rows = share * n
     nc, ny, nz = splits(n)
-    width = 512
+    width = 256
     while out_cols % width:
         width //= 2
     chunks = out_cols // width
@@ -260,32 +416,68 @@
     bf, f32 = jnp.bfloat16, jnp.float32
     dma = pltpu.SemaphoreType.DMA
     vmem = pl.BlockSpec(memory_space=pltpu.VMEM)
+    hbm = pl.BlockSpec(memory_space=pl.ANY)
+    scratch = [
+        pltpu.VMEM((nc, total_rows // nc, 2 * depth), bf),
+        pltpu.VMEM((n, 1, total_rows), f32),
+        pltpu.VMEM((chunks, groups, share, width), bf),
+        pltpu.VMEM((chunks, groups, share, width), bf),
+        pltpu.VMEM((2, groups, share, width), f32),
+        pltpu.VMEM((chunks, nz, share, width), bf),
+        pltpu.VMEM((chunks, nz, share, width), bf),
+        pltpu.VMEM((2, nz, share, width), f32),
+        pltpu.VMEM((chunks, nz, share, width), bf),
+        pltpu.VMEM((chunks, nz, share, width), bf),
+        pltpu.VMEM((2, share, width), f32),
+        dma((n,)),
+        dma((n,)),
+        dma((chunks,)),
+        dma((chunks,)),
+        dma((chunks,)),
+        dma((chunks,)),
+        dma((chunks, nz)),
+        dma((chunks, nz)),
+    ]
+    gain = gain.reshape(1, depth)
+    if fused:
+        half = front[2].shape[0]
+        whole = pltpu.VMEM((total_rows, depth), bf)
+        scratch = [
+            whole,
+            whole,
+            whole,
+            pltpu.VMEM((half, depth), bf),
+            pltpu.VMEM((n, share, w_out.shape[0]), bf),
+            dma((2, nz)),
+            dma((2, nz)),
+            dma((nz,)),
+            dma((nz,)),
+            dma((nz, ny)),
+            dma((nz, ny)),
+            dma((nz,)),
+            dma((nz,)),
+            dma,
+            dma,
+            pltpu.VMEM(w_feat.shape, bf),
+            pltpu.VMEM(w_emb.shape, bf),
+            dma((2,)),
+        ] + scratch
+        args = (*front, gain, w_out, w_feat, w_emb)
+        specs = [vmem] * 5 + [hbm] * 2
+    else:
+        args = (*front, gain, w_feat, w_emb)
+        specs = [vmem] * 6
     return pl.pallas_call(
-        functools.partial(draft_kernel, n, width, chunks, depth * n),
-        out_shape=jax.ShapeDtypeStruct((share, out_cols), bf),
-        in_specs=[vmem] * 6,
-        out_specs=vmem,
-        scratch_shapes=[
-            pltpu.VMEM((nc, total_rows // nc, 2 * depth), bf),
-            pltpu.VMEM((n, 1, total_rows), f32),
-            pltpu.VMEM((chunks, groups, share, width), bf),
-            pltpu.VMEM((chunks, groups, share, width), bf),
-            pltpu.VMEM((2, groups, share, width), f32),
-            pltpu.VMEM((chunks, nz, share, width), bf),
-            pltpu.VMEM((chunks, nz, share, width), bf),
-            pltpu.VMEM((2, nz, share, width), f32),
-            pltpu.VMEM((chunks, nz, share, width), bf),
-            pltpu.VMEM((chunks, nz, share, width), bf),
-            pltpu.VMEM((2, share, width), f32),
-            dma((n,)),
-            dma((n,)),
-            dma((chunks,)),
-            dma((chunks,)),
-            dma((chunks,)),
-            dma((chunks,)),
-            dma((chunks, nz)),
-            dma((chunks, nz)),
-        ],
+        functools.partial(
+            fused_kernel if fused else draft_kernel, n, width, chunks, depth * n
+        ),
+        out_shape=(
+            jax.ShapeDtypeStruct((share, out_cols), bf),
+            jax.ShapeDtypeStruct((total_rows, depth), bf),
+        ),
+        in_specs=specs,
+        out_specs=(vmem, vmem),
+        scratch_shapes=scratch,
         compiler_params=pltpu.CompilerParams(
             collective_id=0, has_side_effects=True, vmem_limit_bytes=VMEM_LIMIT
         ),
@@ -294,7 +486,7 @@
             bytes_accessed=4 * depth * out_cols,
             transcendentals=0,
         ),
-    )(own, other, emb, gain.reshape(1, depth), w_feat, w_emb)
+    )(*args)
 
 
 def swap(value):
@@ -306,31 +498,43 @@
     token_ids, accepted, lengths, queries, new_kv, cache_kv, table, w_out, gain, w_feat, w_emb
 ):
     rows, _, steps = token_ids.shape
-    all_ids = lax.all_gather(token_ids.reshape(-1), "batch", axis=0, tiled=True)
+    share = rows * 2 * steps
+    lanes = -(-share // 128) * 128
+    ids = jnp.pad(token_ids.reshape(1, share), ((0, 7), (0, lanes - share)))
+    all_ids = lax.all_gather(ids, "batch", axis=0, tiled=True)
+    all_ids = all_ids.reshape(n, 8, lanes)[:, 0, :share].reshape(-1)
     vocab_rows = table.shape[0]
     base = lax.axis_index("heads") * vocab_rows
-    local_ids = all_ids - base
-    inside = (local_ids >= 0) & (local_ids < vocab_rows)
-    picked = jnp.take(table, jnp.clip(local_ids, 0, vocab_rows - 1), axis=0)
-    partial_emb = jnp.where(inside[:, None], picked, jnp.bfloat16(0.0))
+
+    def lookup(some):
+        local_ids = some - base
+        inside = (local_ids >= 0) & (local_ids < vocab_rows)
+        picked = jnp.take(table, jnp.clip(local_ids, 0, vocab_rows - 1), axis=0)
+        return jnp.where(inside[:, None], picked, jnp.bfloat16(0.0))
+
+    attn = attend_local(queries, new_kv, cache_kv, lengths, accepted)
     if nh == 2:
-        emb = jnp.where(inside[:, None], picked, swap(partial_emb))
+        half = n * share // 2
+        first = lookup(all_ids[:half])
+        held = swap(first)
+        first_emb = first + held
+        later, first = lax.optimization_barrier((all_ids[half:], first))
+        second = lookup(later)
+        draft, hidden = draft_local(
+            (attn, first_emb, second), gain, w_feat, w_emb, n, w_out
+        )
     else:
-        emb = lax.psum(partial_emb, "heads")
-    attn = attend_local(queries, new_kv, cache_kv, lengths, accepted)
-    proj = jnp.dot(
-        lax.all_gather(attn, "batch", axis=0, tiled=True), w_out, preferred_element_type=jnp.float32
-    )
-    if nh == 2:
-        own = proj.astype(jnp.bfloat16)
-        other = swap(own)
-    else:
+        emb = lax.psum(lookup(all_ids), "heads")
+        proj = jnp.dot(
+            lax.all_gather(attn, "batch", axis=0, tiled=True),
+            w_out,
+            preferred_element_type=jnp.float32,
+        )
         proj = lax.psum(proj, "heads")
         own = proj.astype(jnp.bfloat16)
         other = (proj - own.astype(jnp.float32)).astype(jnp.bfloat16)
-    hidden = emb.astype(jnp.float32) + (own.astype(jnp.float32) + other.astype(jnp.float32))
-    draft = draft_local(own, other, emb, gain, w_feat, w_emb, n)
-    return (hidden.astype(jnp.bfloat16), draft.reshape(rows, 2, steps, w_feat.shape[1]))
+        draft, hidden = draft_local((own, other, emb), gain, w_feat, w_emb, n)
+    return (hidden, draft.reshape(rows, 2, steps, w_feat.shape[1]))
 
 
 def solution(mesh):

time: 226 us -> 229 us (1.013)
  Pallas kernels: 99.1 us -> 156 us
  waiting for transfers between devices: 47.5 us -> 0.01 us
  between operations: 14.8 us -> 0.79 us
  local copies, waits for them, and re-layouts: 34.3 us -> 45.8 us
  blocking collectives: 14.2 us -> 23.3 us
  matrix products: 5.36 us -> 0 us
  starting transfers between devices: 5.06 us -> 0.07 us
  other arithmetic: 5.81 us -> 2.44 us
    pallas_call x1, Pallas kernels: 83.6 us -> 140 us  [draft_local(): pl.pallas_call(functools.partial(fused_kernel if fused else draft_kernel,...]
    ppermute x2 -> x1, waiting for transfers between devices: 34.3 us -> 0.01 us  [swap(): return lax.ppermute(value, 'heads', [(0, 1), (1, 0)])]
    all_gather x0 -> x1, blocking collectives: none -> 23.3 us  [body(): all_ids = lax.all_gather(ids, 'batch', axis=0, tiled=True)]
    unnamed x1 -> x0, blocking collectives: 14.2 us -> none
    all_gather x1 -> x0, waiting for transfers between devices: 13.1 us -> none  [body(): lax.all_gather(attn, 'batch', axis=0, tiled=True)]
    gather x1 -> x2, local copies, waits for them, and re-layouts: 24.4 us -> 36.7 us  [lookup(): picked = jnp.take(table, jnp.clip(local_ids, 0, vocab_rows - 1), axis=0)]
    dot_general x1 -> x0, matrix products: 5.36 us -> none  [body(): jnp.dot(lax.all_gather(attn, 'batch', axis=0, tiled=True), w_out, preferr...]
    ppermute x2 -> x1, starting transfers between devices: 5.02 us -> 0.07 us  [swap(): return lax.ppermute(value, 'heads', [(0, 1), (1, 0)])]
  transfers between devices with their start and end apart: 3 -> 1, of which waited for: 3 -> 0; matrix products, arithmetic and copies ran while one was open for 14% -> 10% of each run, Pallas kernels for 0% -> 7%
where the time goes in v2:
time: 229 us; the launch traced here: 228 us
  Pallas kernels  156 us (68%)
  local copies, waits for them, and re-layouts  45.8 us (20%)
  blocking collectives  23.3 us (10%)
  other arithmetic  2.44 us (1%)
    pallas_call x1, Pallas kernels, draft_local(): pl.pallas_call(functools.partial(fused_kernel if fused else draft_kernel,...  140 us
    gather x2, local copies, waits for them, and re-layouts, lookup(): picked = jnp.take(table, jnp.clip(local_ids, 0, vocab_rows - 1), axis=0)  36.7 us
    all_gather x1, blocking collectives, body(): all_ids = lax.all_gather(ids, 'batch', axis=0, tiled=True)  23.3 us
    pallas_call x1, Pallas kernels, attend_local(): pl.pallas_call(functools.partial(attend_kernel, steps, group, kv_heads),...  15.5 us
  transfers between devices with their start and end apart: 1, of which 0 were waited for; matrix products, arithmetic and copies ran while one was open for 10% of the time, Pallas kernels for 7%

profile of v2, /device:TPU:0, one launch (start us, length us, event | category | flops | bytes accessed | tf_op | source)
XLA Modules:
  0.0 228.4 jit_solution(1072139635280122873)
XLA Ops:
  0.7 0.8 copy.22
  1.5 0.1 reshape.62
  1.6 23.3 %all_gather.3 = s32[128,128]{1,0:T(8,128)S(1)} all-gather(s32[8,128]{1,0:T(8,128)S(1)} %pad.9), channel_id=1, replica_groups=mesh['batch'=16,'heads'=2] {'batch'}, dimensions={0}, use_global_device_ids=true | all-gather | bytes 69632 | tf_op jit(solution)/shard_map/all_gather | solution.py:504
  24.9 0.1 min.18
  25.0 0.1 and.19
  25.1 18.7 %gather_fusion = bf16[640,512]{1,0:T(8,128)(2,1)S(1)} fusion(bf16[32768,512]{1,0:T(8,128)(2,1)} %param.19, s32[1024]{0:T(1024)S(1)} %pad_clamp_fusion.1), kind=kCustom, calls=%fused_computation.clone | custom fusion | bytes 1313280 | tf_op jit(solution)/shard_map/jit(_take)/gather | solution.py:512
  43.8 0.2 select_select_fusion.1
  44.1 0.1 collective-permute-start
  44.1 0.1 slice.15
  44.2 0.1 copy.20
  44.3 0.1 copy.17
  44.4 0.9 copy.18
  45.3 0.7 pad.8.new_ref
  46.0 15.5 %shard_map.122 = bf16[8,4,40,128]{3,2,1,0:T(8,128)(2,1)} custom-call(s32[8]{0:T(128)} %len_ref.1, s32[8]{0:T(128)} %acc_ref.1, bf16[8,4,40,128]{3,2,1,0:T(8,128)(2,1)} %bitcast.18, bf16[8,2,512,512]{3,2,1,0:T(8,128)(2,1)} %kv_ref.1, bf16[8,2,16,512]{3,2,1,0:T(8,128)(2,1)} %pad.8.new_ref), custom_call_target="tpu_custom_call" | custom-call | flops 335544320 | bytes 8388608 | tf_op jit(solution)/shard_map/pallas_call | solution.py:66
  61.5 1.1 copy.27
  62.6 1.0 reshape.61.refs_0_
  63.6 18.0 %gather_fusion.1 = bf16[640,512]{1,0:T(8,128)(2,1)S(1)} fusion(bf16[32768,512]{1,0:T(8,128)(2,1)} %param.19, s32[1024]{0:T(1024)S(1)} %pad_clamp_fusion), kind=kCustom, calls=%fused_computation.1.clone | custom fusion | bytes 1313280 | tf_op jit(solution)/shard_map/jit(_take)/gather | solution.py:512
  81.6 1.1 select_select_fusion.refs_2_
  82.7 0.0 collective-permute-done
  82.7 1.1 fusion.refs_1_
  83.8 140.5 %shard_map.123 = (bf16[80,4096]{1,0:T(8,128)(2,1)}, bf16[1280,512]{1,0:T(8,128)(2,1)}) custom-call(bf16[80,2048]{1,0:T(8,128)(2,1)} %reshape.61.refs_0_, bf16[640,512]{1,0:T(8,128)(2,1)} %fusion.refs_1_, bf16[640,512]{1,0:T(8,128)(2,1)} %select_select_fusion.refs_2_, f32[1,512]{1,0:T(1,128)} %bitcast.26, bf16[2048,512]{1,0:T(8,128)(2,1)} %refs_4_.1, ...), custom_call_target="tpu_custom_call" | custom-call | flops 10737418240 | bytes 8388608 | tf_op jit(solution)/shard_map/pallas_call | solution.py:470
  224.3 1.5 reshape.65
  225.7 1.6 copy.24
  227.3 1.1 copy.29
  (16 shorter events, 0.1 us)
Async XLA Ops:
  0.6 43.6 %copy-start.2 = (bf16[8,2,2,5,512]{4,2,3,1,0:T(2,128)(2,1)S(1)}, bf16[8,2,2,5,512]{4,2,3,1,0:T(2,128)(2,1)}, u32[]{:S(2)}) copy-start(bf16[8,2,2,5,512]{4,2,3,1,0:T(2,128)(2,1)} %param.17) | copy-start | bytes 491524
  0.6 43.7 %copy-start.1 = (bf16[8,2,5,2048]{3,1,2,0:T(2,128)(2,1)S(1)}, bf16[8,2,5,2048]{3,1,2,0:T(2,128)(2,1)}, u32[]{:S(2)}) copy-start(bf16[8,2,5,2048]{3,1,2,0:T(2,128)(2,1)} %param.16) | copy-start | bytes 983044
  44.1 38.6 %collective-permute-start = (bf16[640,512]{1,0:T(8,128)(2,1)S(1)}, bf16[640,512]{1,0:T(8,128)(2,1)S(1)}, u32[]{:S(2)}, u32[]{:S(2)}) collective-permute-start(bf16[640,512]{1,0:T(8,128)(2,1)S(1)} %select_select_fusion.1), channel_id=1, source_target_pairs={{0,1},{1,0},{2,3},{3,2},{4,5},{5,4},{6,7},{7,6},{8,9},{9,8},{10,11... | collective-permute-start | bytes 1966088 | tf_op jit(solution)/shard_map/ppermute | solution.py:493
  224.3 3.1 %copy-start = (bf16[1280,512]{1,0:T(8,128)(2,1)S(1)}, bf16[1280,512]{1,0:T(8,128)(2,1)}, u32[]{:S(2)}) copy-start(bf16[1280,512]{1,0:T(8,128)(2,1)} %get-tuple-element.20) | copy-start | bytes 3932164
